TPU v7x, 512 devices: a whole 4x8x8 slice. The times are simulated.
512 devices in a mesh: panel: 32 (over y, z_lo), col: 8 (over z_hi, x), layer: 2 (over core).
Axes of the slice: x: 4, y: 8, z: 8 (z_hi: 2, z_lo: 4; z = z_hi * 4 + z_lo), core: 2. Of those that a mesh axis runs over, the one named last changes fastest.
Arguments:
- iterate: bfloat16 [8192, 4096], P(('layer', 'panel'), 'col'), parts along dimension 0, may hold values from -3 to 3
Outputs:
- next_iterate: bfloat16 [8192, 4096], P(('layer', 'panel'), 'col'), parts along dimension 0
There are 2 independent parts, one for each index of `layer`. A program takes and returns all parts, laid end to end along the dimension named above; each array names one. Nothing has to cross between parts.
All inputs are finite; a program needn't handle non-finite values.
Results may differ from a plain program's by a relative error of at most 0.015.
Values may be sent and summed in bfloat16 or wider, within the bound.
A program may use at most 64 MiB of HBM per device.

v0:
```python
import jax
import jax.numpy as jnp
from jax import lax
from jax.sharding import PartitionSpec as P


def column_total(partial_value, factor):
    return (
        lax.psum(partial_value.astype(jnp.bfloat16), "col").astype(jnp.float32) * factor
    ).astype(jnp.bfloat16)


def body(iterate):
    cols_dev = iterate.shape[1]
    factor = 1.0 / (cols_dev * lax.axis_size("col"))
    block = lax.dot_general(
        iterate,
        lax.all_gather(iterate, "panel", axis=0, tiled=True),
        (((1,), (1,)), ((), ())),
        preferred_element_type=jnp.float32,
    )
    gram = column_total(block, factor)

    def product_step(panel_rows):
        return jnp.dot(gram, panel_rows, preferred_element_type=jnp.float32)

    first = product_step(lax.all_gather(iterate, "panel", axis=0, tiled=True))
    first_rounded = first.astype(jnp.bfloat16)
    second = product_step(lax.all_gather(first_rounded, "panel", axis=0, tiled=True))
    result = 3.4445 * iterate.astype(jnp.float32) - 4.775 * first + 2.0315 * second
    return result.astype(jnp.bfloat16)


def solution(mesh):
    return jax.shard_map(
        body,
        mesh=mesh,
        in_specs=(P(("layer", "panel"), "col"),),
        out_specs=P(("layer", "panel"), "col"),
        check_vma=False,
    )
```

profile of v0, /device:TPU:6, one launch (start us, length us, event | category | flops | bytes accessed | tf_op | source)
XLA Modules:
  0.0 468.7 jit_solution(2359631505640795663)
XLA Ops:
  6.5 0.0 all-gather.3.cloned.1.call-start
  6.5 0.7 all-gather.3.cloned.1.call-update
  7.3 0.0 all-reduce.2.cloned.1.call-start
  7.3 167.1 %all-gather.3.cloned.1.call-done = bf16[4096,512]{1,0:T(8,128)(2,1)} async-done(((bf16[128,512]{1,0:T(8,128)(2,1)}), bf16[4096,512]{1,0:T(8,128)(2,1)}) %all-gather.3.cloned.1.call-update) | async-done | bytes 4194320 | tf_op jit(solution)/shard_map/all_gather | solution.py:18
  174.4 4.7 %convolution_convert_fusion = bf16[128,4096]{1,0:T(8,128)(2,1)} fusion(bf16[128,512]{1,0:T(8,128)(2,1)} %param.1, bf16[4096,512]{1,0:T(8,128)(2,1)} %all-gather.3.cloned.1.call-done), kind=kOutput, calls=%fused_computation | convolution fusion | flops 537395200 | bytes 5373952 | tf_op jit(solution)/shard_map/dot_general | solution.py:16
  179.2 0.0 copy-start.1
  179.2 0.0 all-reduce.2.cloned.1.call-update
  179.2 0.0 all-gather.5.cloned.1.call-start
  179.2 117.3 %all-reduce.2.cloned.1.call-done = bf16[128,4096]{1,0:T(8,128)(2,1)} async-done(((bf16[128,4096]{1,0:T(8,128)(2,1)}), bf16[128,4096]{1,0:T(8,128)(2,1)}) %all-reduce.2.cloned.1.call-update) | async-done | bytes 1048592 | tf_op jit(solution)/shard_map/psum | solution.py:9
  296.5 0.0 copy-start
  296.5 4.0 fusion.5
  300.5 0.0 all-gather.5.cloned.1.call-update
  300.5 158.1 %all-gather.5.cloned.1.call-done = bf16[4096,512]{1,0:T(8,128)(2,1)} async-done(((bf16[128,512]{1,0:T(8,128)(2,1)}), bf16[4096,512]{1,0:T(8,128)(2,1)}) %all-gather.5.cloned.1.call-update) | async-done | bytes 4194320 | tf_op jit(solution)/shard_map/all_gather | solution.py:29
  458.6 0.0 copy-done.1
  458.6 0.0 copy-done
  458.6 3.6 fusion.1
Async XLA Ops:
  6.5 167.9 %all-gather.3.cloned.1.call-start = ((), (), s32[]{:S(2)}) async-start(), calls=%async_computation | async-start | bytes 4325376 | tf_op jit(solution)/shard_map/all_gather | solution.py:18
  7.3 289.3 %all-reduce.2.cloned.1.call-start = ((), (), s32[]{:S(2)}) async-start(), calls=%async_computation.1 | async-start | bytes 2097152 | tf_op jit(solution)/shard_map/psum | solution.py:9
  179.2 279.5 %copy-start.1 = (bf16[128,512]{1,0:T(8,128)(2,1)S(1)}, bf16[128,512]{1,0:T(8,128)(2,1)}, u32[]{:S(2)}) copy-start(bf16[128,512]{1,0:T(8,128)(2,1)} %param.1) | copy-start | bytes 393220
  179.2 279.4 %all-gather.5.cloned.1.call-start = ((), (), s32[]{:S(2)}) async-start(), calls=%async_computation.2 | async-start | bytes 4325376 | tf_op jit(solution)/shard_map/all_gather | solution.py:29
  296.5 162.1 %copy-start = (bf16[128,4096]{1,0:T(8,128)(2,1)S(1)}, bf16[128,4096]{1,0:T(8,128)(2,1)}, u32[]{:S(2)}) copy-start(bf16[128,4096]{1,0:T(8,128)(2,1)} %all-reduce.2.cloned.1.call-done) | copy-start | bytes 3145732
Sparse Core Ops, SparseCore 0:
  9.4 164.9 all-gather.2
  179.3 117.1 all-reduce.1
  300.7 157.9 all-gather.4
where the time goes:
time: 469 us
  waiting for transfers between devices  443 us (94%)
  between operations  13.1 us (3%)
  matrix products  12.3 us (3%)
    all_gather x1, waiting for transfers between devices, body(): lax.all_gather(iterate, 'panel', axis=0, tiled=True)  167 us
    all_gather x1, waiting for transfers between devices, body(): lax.all_gather(first_rounded, 'panel', axis=0, tiled=True)  158 us
    psum x1, waiting for transfers between devices, column_total(): lax.psum(partial_value.astype(jnp.bfloat16), 'col').astype(jnp.float32)  117 us
  transfers between devices with their start and end apart: 3, of which 3 were waited for; matrix products, arithmetic and copies ran while one was open for 0% of the time, Pallas kernels for 0%

commit v1 on v0

v1 whole, which is shorter than its diff:
```python
import functools

import jax
import jax.numpy as jnp
from jax import lax
from jax.experimental import pallas as pl
from jax.experimental.pallas import tpu as pltpu
from jax.sharding import PartitionSpec as P

NX, N, NLO = 4, 8, 4
HALF = N // 2
ROWS, COLS = 64, 1024
MESH = pl.DeviceIdType.MESH
UPTO = 99


def kernel(x_ref, o_ref, w, p, q, gp, gr, g, fp, fr, f, sp, sr, first, ow,
           ex_sem, p_sem, q_sem, gr_sem, g_sem, fr_sem, f_sem, sr_sem, out_sem):
    panel, col, layer = lax.axis_index("panel"), lax.axis_index("col"), lax.axis_index("layer")
    y, z_lo = panel // NLO, panel % NLO
    z_hi, x = col // NX, col % NX
    z = z_hi * NLO + z_lo

    def device(x, y, z):
        return (y * NLO + z % NLO, (z // NLO) * NX + x, layer)

    def peer1(d):
        return device(x, (y + d * layer) % N, (z + d * (1 - layer)) % N)

    def peer2(d):
        return device(x, (y + d * (1 - layer)) % N, (z + d * layer) % N)

    def peer_x(d):
        return device((x + d) % NX, y, z)

    partner = device(x, y, (z + HALF) % N)
    pos1 = z * (1 - layer) + y * layer
    pos2 = y * (1 - layer) + z * layer

    barrier = pltpu.get_barrier_semaphore()
    for d in range(1, N):
        pl.semaphore_signal(barrier, inc=1, device_id=peer1(d), device_id_type=MESH)
        pl.semaphore_signal(barrier, inc=1, device_id=peer2(d), device_id_type=MESH)
    for d in range(1, NX):
        pl.semaphore_signal(barrier, inc=1, device_id=peer_x(d), device_id_type=MESH)
    pl.semaphore_wait(barrier, 2 * (N - 1) + NX - 1)

    def send(src, dst, sems, k, to):
        copy = pltpu.make_async_remote_copy(
            src_ref=src, dst_ref=dst, send_sem=sems.at[0, k], recv_sem=sems.at[1, k],
            device_id=to, device_id_type=MESH)
        copy.start()
        return copy

    started = []

    mine = pl.multiple_of(z_hi * ROWS, ROWS)
    other = pl.multiple_of((1 - z_hi) * ROWS, ROWS)
    mine_c = pl.multiple_of(z_hi * 512, 512)
    other_c = pl.multiple_of((1 - z_hi) * 512, 512)
    if UPTO >= 1:
        ex = send(x_ref.at[pl.ds(other, ROWS), :], w.at[:, pl.ds(mine_c, 512)], ex_sem, 0, partner)
        w[:, pl.ds(mine_c, 512)] = x_ref[pl.ds(mine, ROWS), :]
        ex.wait()

    def gather_steps(src, buf, sems, pos, peer):
        right, left = peer(1), peer(N - 1)
        prev = None
        for s in range(1, HALF + 1):
            if prev is not None:
                prev[0].wait_recv()
            a = src if s == 1 else buf.at[(pos + N - s + 1) % N]
            da = buf.at[(pos + N - s + 1) % N]
            b = src if s == 1 else buf.at[(pos + s - 1) % N]
            db = buf.at[(pos + s - 1) % N]
            if s == HALF:
                a, da = a.at[pl.ds(0, ROWS // 2), :], da.at[pl.ds(0, ROWS // 2), :]
                b, db = b.at[pl.ds(ROWS // 2, ROWS // 2), :], db.at[pl.ds(ROWS // 2, ROWS // 2), :]
            ca = send(a, da, sems, 2 * s - 2, right)
            if prev is not None:
                prev[1].wait_recv()
            cb = send(b, db, sems, 2 * s - 1, left)
            prev = (ca, cb)
            started.extend(prev)
            yield
        prev[0].wait_recv()
        prev[1].wait_recv()
        yield

    def run(*gens):
        gens = list(gens)
        for _ in range(HALF + 1):
            for gen in gens:
                next(gen)

    if UPTO >= 2:
        run(gather_steps(w, p, p_sem, pos1, peer1), gather_steps(w, q, q_sem, pos2, peer2))
        p[pos1] = w[...]
        q[pos2] = w[...]

    if UPTO >= 3:
        pm = p[...].reshape(N * ROWS, COLS)
        qm = q[...].reshape(N * ROWS, COLS)
        gp[...] = lax.dot_general(pm, qm, (((1,), (1,)), ((), ())), preferred_element_type=jnp.float32
                                  ).astype(jnp.bfloat16).reshape(gp.shape)
        copies = [send(gp.at[(x + d) % NX], gr.at[d - 1], gr_sem, d - 1, peer_x(d)) for d in range(1, NX)]
        total = gp[x].astype(jnp.float32)
        for d, c in enumerate(copies):
            c.wait_recv()
            total += gr[d].astype(jnp.float32)
        started.extend(copies)
        g[x] = (total * (1.0 / 4096)).astype(jnp.bfloat16)
    if UPTO >= 4:
        copies = [send(g.at[x], g.at[x], g_sem, d - 1, peer_x(d)) for d in range(1, NX)]
        for c in copies:
            c.wait_recv()
        started.extend(copies)

    def scatter(parts, got, sems, pos, peer):
        copies = [send(parts.at[(pos + d) % N], got.at[d - 1], sems, d - 1, peer(d)) for d in range(1, N)]
        total = parts[pos].astype(jnp.float32)
        for d, c in enumerate(copies):
            c.wait_recv()
            total += got[d].astype(jnp.float32)
        started.extend(copies)
        return total

    if UPTO >= 5:
        gm = g[...].reshape(N * ROWS, N * ROWS)
        fp[...] = jnp.dot(gm, q[...].reshape(N * ROWS, COLS), preferred_element_type=jnp.float32
                          ).astype(jnp.bfloat16).reshape(fp.shape)
        first[...] = scatter(fp, fr, fr_sem, pos1, peer1)
        f[pos1] = first[...].astype(jnp.bfloat16)
    if UPTO >= 6:
        run(gather_steps(f.at[pos1], f, f_sem, pos1, peer1))
    if UPTO >= 7:
        gm = g[...].reshape(N * ROWS, N * ROWS)
        fm = f[...].reshape(N * ROWS, COLS)
        sp[...] = lax.dot_general(gm, fm, (((0,), (0,)), ((), ())), preferred_element_type=jnp.float32
                                  ).astype(jnp.bfloat16).reshape(sp.shape)
        second = scatter(sp, sr, sr_sem, pos2, peer2)
        ow[...] = (3.4445 * w[...].astype(jnp.float32) - 4.775 * first[...] + 2.0315 * second).astype(jnp.bfloat16)
    if UPTO >= 8:
        out = send(ow.at[:, pl.ds(other_c, 512)], o_ref.at[pl.ds(mine, ROWS), :], out_sem, 0, partner)
        o_ref[pl.ds(mine, ROWS), :] = ow[:, pl.ds(mine_c, 512)]
        out.wait()
    else:
        o_ref[...] = x_ref[...]
    for c in started:
        c.wait_send()


def body(iterate):
    bf, f32 = jnp.bfloat16, jnp.float32
    stack = pltpu.VMEM((N, ROWS, COLS), bf)
    gram = pltpu.VMEM((NX, N * ROWS // NX, N * ROWS), bf)
    dma = lambda n: pltpu.SemaphoreType.DMA((2, n))
    return pl.pallas_call(
        kernel,
        out_shape=jax.ShapeDtypeStruct(iterate.shape, bf),
        in_specs=[pl.BlockSpec(memory_space=pltpu.VMEM)],
        out_specs=pl.BlockSpec(memory_space=pltpu.VMEM),
        scratch_shapes=[
            pltpu.VMEM((ROWS, COLS), bf), stack, stack,
            gram, pltpu.VMEM((NX - 1, N * ROWS // NX, N * ROWS), bf), gram,
            stack, pltpu.VMEM((N - 1, ROWS, COLS), bf), stack,
            stack, pltpu.VMEM((N - 1, ROWS, COLS), bf),
            pltpu.VMEM((ROWS, COLS), f32), pltpu.VMEM((ROWS, COLS), bf),
            dma(1), dma(N), dma(N), dma(NX - 1), dma(NX - 1), dma(N - 1), dma(N), dma(N - 1), dma(1),
        ],
        compiler_params=pltpu.CompilerParams(
            collective_id=0, has_side_effects=True, vmem_limit_bytes=40 * 1024 * 1024),
    )(iterate)


def solution(mesh):
    return jax.shard_map(
        body, mesh=mesh,
        in_specs=(P(("layer", "panel"), "col"),),
        out_specs=P(("layer", "panel"), "col"),
        check_vma=False,
    )
```

time: 469 us -> 118 us (0.25)
  the two profiles are of different devices: /device:TPU:6 before, /device:TPU:4 now
where the time goes in v1:
time: 118 us; the launch traced here: 117 us
  Pallas kernels  116 us (98%)
  local copies, waits for them, and re-layouts  1.56 us (1%)
    pallas_call x1, Pallas kernels, body(): pl.pallas_call(kernel, out_shape=jax.ShapeDtypeStruct(iterate.shape, bf),...  116 us

profile of v1, /device:TPU:4, one launch (start us, length us, event | category | flops | bytes accessed | tf_op | source)
XLA Modules:
  0.0 117.4 jit_solution(9575317823369298793)
XLA Ops:
  0.0 0.0 copy-start
  0.0 0.9 copy-done
  0.9 115.9 %shard_map.17 = bf16[128,512]{1,0:T(8,128)(2,1)S(1)} custom-call(bf16[128,512]{1,0:T(8,128)(2,1)S(1)} %copy-done), custom_call_target="tpu_custom_call" | custom-call | tf_op jit(solution)/shard_map/pallas_call | solution.py:158
  116.8 0.7 copy.3
Async XLA Ops:
  0.0 0.9 copy-start

commit v2 on v0

v2 whole, which is shorter than its diff:
```python
import jax
import jax.numpy as jnp
from jax import lax
from jax.experimental import pallas as pl
from jax.experimental.pallas import tpu as pltpu
from jax.sharding import PartitionSpec as P

NX, N, NLO = 4, 8, 4
HALF = N // 2
ROWS, COLS = 64, 512
PART = COLS // 2
MESH = pl.DeviceIdType.MESH
BF, F32 = jnp.bfloat16, jnp.float32
UPTO = 99
FLIP = 1


def kernel(x_ref, o_ref, ab, acc, gp, gr, g, gt, fp, fr, f, first, sp, sr0, sr1, ow,
           ex_sem, a_sem, b_sem, gr_sem, g_sem, fr_sem, f_sem, sr_sem, out_sem):
    panel, col, layer = lax.axis_index("panel"), lax.axis_index("col"), lax.axis_index("layer")
    y, z_lo = panel // NLO, panel % NLO
    z_hi, x = col // NX, col % NX
    z = z_hi * NLO + z_lo
    o = 1 - layer if FLIP else layer

    def device(x, y, z):
        return (y * NLO + z % NLO, (z // NLO) * NX + x, layer)

    def unplace(t):
        return (t % 2) * NLO + t // 2

    def ring1(t):
        return device(x, y + o * (t - y), z + (1 - o) * (unplace(t) - z))

    def ring2(t):
        return device(x, y + (1 - o) * (t - y), z + o * (unplace(t) - z))

    def peer_x(d):
        return device((x + d) % NX, y, z)

    placed = z_lo * 2 + z_hi
    own1 = (1 - o) * placed + o * y
    own2 = (1 - o) * y + o * placed
    partner = device(x, y, (z + HALF) % N)

    barrier = pltpu.get_barrier_semaphore()
    for d in range(1, N):
        pl.semaphore_signal(barrier, inc=1, device_id=device(x, (y + d) % N, z), device_id_type=MESH)
        pl.semaphore_signal(barrier, inc=1, device_id=device(x, y, (z + d) % N), device_id_type=MESH)
    for d in range(1, NX):
        pl.semaphore_signal(barrier, inc=1, device_id=peer_x(d), device_id_type=MESH)
    pl.semaphore_wait(barrier, 2 * (N - 1) + NX - 1)

    def remote(src, dst, send_sem, recv_sem, to):
        return pltpu.make_async_remote_copy(
            src_ref=src, dst_ref=dst, send_sem=send_sem, recv_sem=recv_sem, device_id=to, device_id_type=MESH)

    started = []

    def send(src, dst, send_sem, recv_sem, to):
        copy = remote(src, dst, send_sem, recv_sem, to)
        copy.start()
        started.append(copy)
        return copy

    mine = pl.multiple_of(z_hi * ROWS, ROWS)
    other = pl.multiple_of((1 - z_hi) * ROWS, ROWS)

    exchange = send(x_ref.at[pl.ds(other, ROWS), :], ab.at[1 - o, z_hi, y], ex_sem.at[0, 0], ex_sem.at[1, 0], partner)

    sent = {}

    def along(ring, step, u):
        for way in (0, 1):
            if step == HALF and way != u:
                continue
            if step > 1:
                sent[ring, step - 1, u, way].wait_recv()
            back = 1 - step if way == 0 else step - 1
            if ring == 0:
                zz = (z + back + N) % N
                slot = ab.at[o, zz // NLO, (zz % NLO) * 2 + u]
                src = x_ref.at[pl.ds(u * ROWS, ROWS), :] if step == 1 else slot
                to = device(x, y, (z + (1 if way == 0 else N - 1)) % N)
                sems = a_sem
            else:
                yy = (y + back + N) % N
                slot = ab.at[1 - o, z_hi if u == 0 else 1 - z_hi, yy]
                src = x_ref.at[pl.ds(mine, ROWS), :] if step == 1 and u == 0 else slot
                to = device(x, (y + (1 if way == 0 else N - 1)) % N, z)
                sems = b_sem
            k = (step - 1) * 4 + u * 2 + way
            sent[ring, step, u, way] = send(src, slot, sems.at[0, k], sems.at[1, k], to)

    def arrived(ring, u):
        sent[ring, HALF, u, u].wait_recv()
        sent[ring, HALF - 1, u, 1 - u].wait_recv()

    for a in ((0, 1, 0), (1, 1, 0), (0, 1, 1)):
        along(*a)
    for u in (0, 1):
        ab[o, z_hi, z_lo * 2 + u] = x_ref[u * ROWS:(u + 1) * ROWS, :]
    ab[1 - o, z_hi, y] = x_ref[pl.ds(mine, ROWS), :]
    for a in ((0, 2, 0), (1, 2, 0), (0, 2, 1)):
        along(*a)
    exchange.wait_recv()
    for a in ((1, 1, 1), (0, 3, 0), (1, 3, 0), (0, 3, 1), (1, 2, 1), (0, 4, 0), (1, 4, 0), (0, 4, 1), (1, 3, 1), (1, 4, 1)):
        along(*a)
    arrived(0, 0)
    arrived(0, 1)
    arrived(1, 0)

    def nt(a, b):
        return lax.dot_general(a, b, (((1,), (1,)), ((), ())), preferred_element_type=F32)

    rows_all, rows_half = N * ROWS, HALF * ROWS
    acc[...] = nt(ab[0, z_hi].reshape(rows_all, COLS), ab[1, z_hi].reshape(rows_all, COLS))
    arrived(1, 1)

    own_half = own1 // HALF
    halves = (1 - own_half, own_half)
    c_late = 1 - z_hi
    if UPTO >= 3:
        gr_copies = []
        for k, half in enumerate(halves):
            at = pl.multiple_of(half * rows_half, rows_half)
            block = acc[pl.ds(at, rows_half), :] + nt(
                ab[0, c_late, pl.ds(half * HALF, HALF)].reshape(rows_half, COLS), ab[1, c_late].reshape(rows_all, COLS))
            gp[pl.ds(half * HALF, HALF)] = block.astype(BF).reshape(HALF, ROWS, rows_all)
            gr_copies.append([
                send(gp.at[half * HALF + (x + d) % NX], gr.at[k, d - 1], gr_sem.at[0, k * 3 + d - 1],
                     gr_sem.at[1, k * 3 + d - 1], peer_x(d)) for d in (2, 1, 3)])
        g_copies = []
        for k, half in enumerate(halves):
            mine_g = half * HALF + x
            for c in gr_copies[k]:
                c.wait_recv()
            total = gp[mine_g].astype(F32)
            for d in range(NX - 1):
                total += gr[k, d].astype(F32)
            g[mine_g] = (total * (1.0 / 4096)).astype(BF)
            g_copies.append([
                send(g.at[mine_g], g.at[mine_g], g_sem.at[0, k * 3 + d - 1], g_sem.at[1, k * 3 + d - 1], peer_x(d))
                for d in (2, 1, 3)])
    if UPTO >= 5:
        def send_first(v, k, half):
            for e in range(k, HALF):
                t = half * HALF + (own1 + e) % HALF
                send(fp.at[v, t], fr.at[v, own1], fr_sem.at[0, v * N + t], fr_sem.at[1, v * N + own1], ring1(t))

        for k, half in enumerate(halves):
            for c in g_copies[k]:
                c.wait_recv()
            rows = g[pl.ds(half * HALF, HALF)].reshape(rows_half, rows_all)
            for v in (0, 1):
                for c in (0, 1):
                    right = ab[1, c, :, :, v * PART:(v + 1) * PART].reshape(rows_all, PART)
                    fp[v, pl.ds(half * HALF, HALF), :, c * PART:(c + 1) * PART] = jnp.dot(
                        rows, right, preferred_element_type=F32).astype(BF).reshape(HALF, ROWS, PART)
                if v == 0:
                    send_first(v, k, half)
        for k, half in enumerate(halves):
            send_first(1, k, half)
        gt[...] = g[...].reshape(rows_all, rows_all).T

        others1 = [(own1 + e) % N for e in range(1, N)]
        others2 = [(own2 + e) % N for e in range(1, N)]
        for v in (0, 1):
            fr[v, own1] = fp[v, own1]
            for t in others1:
                remote(fr.at[v, t], fr.at[v, t], fr_sem.at[0, v * N + t], fr_sem.at[1, v * N + t], ring1(t)).wait_recv()
            total = fr[v, 0].astype(F32)
            for t in range(1, N):
                total += fr[v, t].astype(F32)
            first[v] = total
            f[v, own1] = total.astype(BF)
            if UPTO >= 6:
                for t in others1:
                    send(f.at[v, own1], f.at[v, own1], f_sem.at[0, v * N + t], f_sem.at[1, v * N + own1], ring1(t))

    if UPTO >= 7:
        rows2 = pl.multiple_of(own2 * ROWS, ROWS)

        def second_copy(v, t, way):
            sems = (sr_sem.at[0, v * N + t], sr_sem.at[1, v * N + own2])
            if way == 0:
                return remote(sp.at[v, t], sr0.at[v, own2], *sems, ring2(t))
            zz = unplace(t)
            return remote(sp.at[v, pl.ds((zz % NLO) * 2, 2), :, pl.ds(pl.multiple_of((zz // NLO) * PART, PART), PART)],
                          sr1.at[v, own2], *sems, ring2(t))

        def second_came(v, t, way):
            slot = (sr0, sr1)[way].at[v, t]
            return remote(slot, slot, sr_sem.at[0, v * N + t], sr_sem.at[1, v * N + t], ring2(t))

        for v in (0, 1):
            for t in others1:
                remote(f.at[v, t], f.at[v, t], f_sem.at[0, v * N + t], f_sem.at[1, v * N + t], ring1(t)).wait_recv()
            second = 2.0315 * jnp.dot(gt[...], f[v].reshape(rows_all, COLS), preferred_element_type=F32)
            sp[v] = second.astype(BF).reshape(N, ROWS, COLS)
            sp[v, own2] = (sp[v, own2].astype(F32) - 4.775 * first[v]).astype(BF)
            for way in (0, 1):
                @pl.when(o == way)
                def _():
                    for t in others2:
                        second_copy(v, t, way).start()
                    if way == 0:
                        sr0[v, own2] = sp[v, own2]
                    else:
                        sr1[v, own2] = sp[v, pl.ds(z_lo * 2, 2), :, pl.ds(pl.multiple_of(z_hi * PART, PART), PART)]

        def out_copy(v):
            return remote(ow.at[v, :, pl.ds(pl.multiple_of((1 - z_hi) * PART, PART), PART)],
                          o_ref.at[pl.ds(mine, ROWS), v * PART:(v + 1) * PART],
                          out_sem.at[0, v], out_sem.at[1, v], partner)

        @pl.when(o == 0)
        def _():
            for v in (0, 1):
                for t in others2:
                    second_came(v, t, 0).wait_recv()
                total = sr0[v, 0].astype(F32)
                for t in range(1, N):
                    total += sr0[v, t].astype(F32)
                for c in (0, 1):
                    own = ab[1, c, y, :, v * PART:(v + 1) * PART]
                    ow[v, :, c * PART:(c + 1) * PART] = (
                        3.4445 * own.astype(F32) + total[:, c * PART:(c + 1) * PART]).astype(BF)
                out_copy(v).start()
                o_ref[pl.ds(mine, ROWS), v * PART:(v + 1) * PART] = ow[
                    v, :, pl.ds(pl.multiple_of(z_hi * PART, PART), PART)]
            for v in (0, 1):
                for t in others2:
                    second_copy(v, t, 0).wait_send()
                out_copy(v).wait()

        @pl.when(o == 1)
        def _():
            for v in (0, 1):
                for t in others2:
                    second_came(v, t, 1).wait_recv()
                for h in (0, 1):
                    total = sr1[v, 0, h].astype(F32)
                    for t in range(1, N):
                        total += sr1[v, t, h].astype(F32)
                    own = x_ref[h * ROWS:(h + 1) * ROWS, v * PART:(v + 1) * PART]
                    o_ref[h * ROWS:(h + 1) * ROWS, v * PART:(v + 1) * PART] = (
                        3.4445 * own.astype(F32) + total).astype(BF)
            for v in (0, 1):
                for t in others2:
                    second_copy(v, t, 1).wait_send()
    else:
        o_ref[...] = x_ref[...]
    for c in started:
        c.wait_send()


def body(iterate):
    stack = pltpu.VMEM((2, N, ROWS, COLS), BF)
    gram = pltpu.VMEM((N, ROWS, N * ROWS), BF)
    dma = lambda n: pltpu.SemaphoreType.DMA((2, n))
    return pl.pallas_call(
        kernel,
        out_shape=jax.ShapeDtypeStruct(iterate.shape, BF),
        in_specs=[pl.BlockSpec(memory_space=pltpu.VMEM)],
        out_specs=pl.BlockSpec(memory_space=pltpu.VMEM),
        scratch_shapes=[
            pltpu.VMEM((2, 2, N, ROWS, COLS), BF),
            pltpu.VMEM((N * ROWS, N * ROWS), F32),
            gram, pltpu.VMEM((2, NX - 1, ROWS, N * ROWS), BF), gram,
            pltpu.VMEM((N * ROWS, N * ROWS), BF),
            stack, stack, stack,
            pltpu.VMEM((2, ROWS, COLS), F32),
            stack, stack, pltpu.VMEM((2, N, 2, ROWS, PART), BF),
            pltpu.VMEM((2, ROWS, COLS), BF),
            dma(1), dma(16), dma(16), dma(6), dma(6), dma(16), dma(16), dma(16), dma(2),
        ],
        compiler_params=pltpu.CompilerParams(
            collective_id=0, has_side_effects=True, vmem_limit_bytes=40 * 1024 * 1024),
    )(iterate)


def solution(mesh):
    return jax.shard_map(
        body, mesh=mesh,
        in_specs=(P(("layer", "panel"), "col"),),
        out_specs=P(("layer", "panel"), "col"),
        check_vma=False,
    )
```

time: 469 us -> 99.9 us (0.21)
  waiting for transfers between devices: 443 us -> 0 us
  Pallas kernels: 0 us -> 98.2 us
  between operations: 13.1 us -> 0.01 us
  matrix products: 12.3 us -> 0 us
    all_gather x2 -> x0, waiting for transfers between devices: 325 us -> none  [the longest x1 167 us: body(): lax.all_gather(iterate, 'panel', axis=0, tiled=True)]
    psum x1 -> x0, waiting for transfers between devices: 117 us -> none  [column_total(): lax.psum(partial_value.astype(jnp.bfloat16), 'col').astype(jnp.float32)]
    pallas_call x0 -> x1, Pallas kernels: none -> 98.2 us  [body(): pl.pallas_call(kernel, out_shape=jax.ShapeDtypeStruct(iterate.shape, BF),...]
    dot_general x3 -> x0, matrix products: 12.3 us -> none  [the longest x2 7.54 us: product_step(): return jnp.dot(gram, panel_rows, preferred_element_type=jnp.float32)]
  transfers between devices with their start and end apart: 3 -> 0, of which waited for: 3 -> 0; matrix products, arithmetic and copies ran while one was open for 0% -> 0% of each run, Pallas kernels for 0% -> 0%
where the time goes in v2:
time: 99.9 us; the launch traced here: 99.7 us
  Pallas kernels  98.2 us (98%)
  local copies, waits for them, and re-layouts  1.56 us (2%)
    pallas_call x1, Pallas kernels, body(): pl.pallas_call(kernel, out_shape=jax.ShapeDtypeStruct(iterate.shape, BF),...  98.2 us

profile of v2, /device:TPU:6, one launch (start us, length us, event | category | flops | bytes accessed | tf_op | source)
XLA Modules:
  0.0 99.7 jit_solution(4555538250879670795)
XLA Ops:
  0.0 0.0 copy-start
  0.0 0.9 copy-done
  0.9 98.2 %shard_map.17 = bf16[128,512]{1,0:T(8,128)(2,1)S(1)} custom-call(bf16[128,512]{1,0:T(8,128)(2,1)S(1)} %copy-done), custom_call_target="tpu_custom_call" | custom-call | tf_op jit(solution)/shard_map/pallas_call | solution.py:262
  99.1 0.7 copy.3
Async XLA Ops:
  0.0 0.9 copy-start

commit v3 on v0

v3 whole, which is shorter than its diff:
```python
import jax
import jax.numpy as jnp
from jax import lax
from jax.experimental import pallas as pl
from jax.experimental.pallas import tpu as pltpu
from jax.sharding import PartitionSpec as P

NX, N, NLO = 4, 8, 4
HALF = N // 2
ROWS, COLS = 64, 512
PART = COLS // 2
MESH = pl.DeviceIdType.MESH
BF, F32 = jnp.bfloat16, jnp.float32


def kernel(x_ref, o_ref, ab, acc, gp, gr, g, gt, fp, fb, fh, fd, fs, f, first, sp, sb, sh, sd, ss, ow,
           ex_sem, a_sem, b_sem, gr_sem, g_sem, fr_sem, f_sem, sr_sem, out_sem):
    panel, col, layer = lax.axis_index("panel"), lax.axis_index("col"), lax.axis_index("layer")
    y, z_lo = panel // NLO, panel % NLO
    z_hi, x = col // NX, col % NX
    z = z_hi * NLO + z_lo
    o = 1 - layer

    def device(x, y, z):
        return (y * NLO + z % NLO, (z // NLO) * NX + x, layer)

    def place(zz):
        return (zz % NLO) * 2 + zz // NLO

    def ring_y(d):
        return device(x, (y + d + N) % N, z)

    def ring_z(d):
        return device(x, y, (z + d + N) % N)

    def ring1(d):
        return device(x, (y + o * d + N) % N, (z + (1 - o) * d + N) % N)

    def ring2(d):
        return device(x, (y + (1 - o) * d + N) % N, (z + o * d + N) % N)

    def place1(d):
        return (1 - o) * place((z + d + N) % N) + o * ((y + d + N) % N)

    def pos2(d):
        return ((1 - o) * y + o * z + d + N) % N

    def peer_x(d):
        return device((x + d) % NX, y, z)

    own1 = place1(0)
    partner = device(x, y, (z + HALF) % N)

    barrier = pltpu.get_barrier_semaphore()
    for d in range(1, N):
        pl.semaphore_signal(barrier, inc=1, device_id=ring_y(d), device_id_type=MESH)
        pl.semaphore_signal(barrier, inc=1, device_id=ring_z(d), device_id_type=MESH)
    for d in range(1, NX):
        pl.semaphore_signal(barrier, inc=1, device_id=peer_x(d), device_id_type=MESH)
    pl.semaphore_wait(barrier, 2 * (N - 1) + NX - 1)

    def remote(src, dst, send_sem, recv_sem, to):
        return pltpu.make_async_remote_copy(
            src_ref=src, dst_ref=dst, send_sem=send_sem, recv_sem=recv_sem, device_id=to, device_id_type=MESH)

    started = []

    def send(src, dst, send_sem, recv_sem, to):
        copy = remote(src, dst, send_sem, recv_sem, to)
        copy.start()
        started.append(copy)
        return copy

    def gather(slot, ring, sems, base, far):
        def one(code, src, d):
            return send(src, src, sems.at[0, base + code], sems.at[1, base + code], ring(d))

        own = slot(0)
        second = [one(0, own, 2), one(1, own, -2)]
        last = [one(2, own, 1), one(3, own, -1)]
        yield
        for way, sign in ((0, 1), (1, -1)):
            second[way].wait_recv()
            passed = slot(-2 * sign)
            part = far(way, passed)
            if part is not None:
                last.append(one(4 + way, part, 2 * sign))
            last.append(one(6 + way, passed, sign))
        yield
        for copy in last:
            copy.wait_recv()
        yield

    def scatter(parts, index, halves, relay, relay_half, direct, sums, ring, sems, base):
        def one(code, src, dst, d):
            return send(src, dst, sems.at[0, base + code], sems.at[1, base + code], ring(d))

        met, last = [], []
        for way, sign in ((0, -1), (1, 1)):
            met.append([one(way, parts.at[index(4 * sign)].at[halves[way]], relay_half.at[way], 2 * sign)])
        for way, sign in ((0, -1), (1, 1)):
            met[way].append(one(2 + way, parts.at[index(3 * sign)], relay.at[way], sign))
        for way, sign in ((0, -1), (1, 1)):
            last.append(one(4 + way, parts.at[index(sign)], direct.at[way], sign))
        yield
        for way, sign in ((0, -1), (1, 1)):
            for copy in met[way]:
                copy.wait_recv()
            sums[way] = (parts[index(2 * sign)].astype(F32) + relay[way].astype(F32)).astype(BF)
            half = halves[way]
            sums.at[way].at[half][...] = (parts.at[index(2 * sign)].at[half][...].astype(F32) + relay.at[way].at[half][...].astype(F32)
                                + relay_half[way].astype(F32)).astype(BF)
            last.append(one(6 + way, sums.at[way], direct.at[2 + way], 2 * sign))
        yield
        total = parts[index(0)].astype(F32)
        for i, copy in enumerate(last):
            copy.wait_recv()
            total += direct[i].astype(F32)
        yield total

    mine = pl.multiple_of(z_hi * ROWS, ROWS)
    other = pl.multiple_of((1 - z_hi) * ROWS, ROWS)

    exchange = send(x_ref.at[pl.ds(other, ROWS), :], ab.at[1 - o, z_hi, y], ex_sem.at[0, 0], ex_sem.at[1, 0], partner)

    def slot_a(u):
        def slot(d):
            zz = (z + d + N) % N
            return ab.at[o, zz // NLO, (zz % NLO) * 2 + u]
        return slot

    def slot_b(c):
        return lambda d: ab.at[1 - o, c, (y + d + N) % N]

    def one_way(u):
        return lambda way, ref: ref if way == u else None

    c_late = 1 - z_hi
    a0 = gather(slot_a(0), ring_z, a_sem, 0, one_way(0))
    a1 = gather(slot_a(1), ring_z, a_sem, 8, one_way(1))
    b0 = gather(slot_b(z_hi), ring_y, b_sem, 0, one_way(0))
    b1 = gather(slot_b(c_late), ring_y, b_sem, 8, one_way(1))
    ab[1 - o, z_hi, y] = x_ref[pl.ds(mine, ROWS), :]
    next(b0)
    for u in (0, 1):
        ab[o, z_hi, z_lo * 2 + u] = x_ref[u * ROWS:(u + 1) * ROWS, :]
    next(a0)
    next(a1)
    next(b0)
    next(a0)
    exchange.wait_recv()
    next(b1)
    next(a1)
    next(b1)
    next(b0)
    next(a0)
    next(a1)

    def nt(a, b):
        return lax.dot_general(a, b, (((1,), (1,)), ((), ())), preferred_element_type=F32)

    rows_all, rows_half = N * ROWS, HALF * ROWS
    acc[...] = nt(ab[0, z_hi].reshape(rows_all, COLS), ab[1, z_hi].reshape(rows_all, COLS))
    next(b1)

    gr_copies = []
    for k in (0, 1):
        block = acc[k * rows_half:(k + 1) * rows_half, :] + nt(
            ab[0, c_late, k * HALF:(k + 1) * HALF].reshape(rows_half, COLS), ab[1, c_late].reshape(rows_all, COLS))
        gp[k * HALF:(k + 1) * HALF] = block.astype(BF).reshape(HALF, ROWS, rows_all)
        gr_copies.append([
            send(gp.at[k * HALF + (x + d) % NX], gr.at[k, d - 1], gr_sem.at[0, k * 3 + d - 1],
                 gr_sem.at[1, k * 3 + d - 1], peer_x(d)) for d in (2, 1, 3)])
    g_copies = []
    for k in (0, 1):
        mine_g = k * HALF + x
        for c in gr_copies[k]:
            c.wait_recv()
        total = gp[mine_g].astype(F32)
        for d in range(NX - 1):
            total += gr[k, d].astype(F32)
        g[mine_g] = (total * (1.0 / 4096)).astype(BF)
        g_copies.append([
            send(g.at[mine_g], g.at[mine_g], g_sem.at[0, k * 3 + d - 1], g_sem.at[1, k * 3 + d - 1], peer_x(d))
            for d in (2, 1, 3)])

    row_halves = (pl.ds(0, ROWS // 2), pl.ds(ROWS // 2, ROWS // 2))
    firsts = [scatter(fp.at[v], place1, row_halves, fb.at[v], fh.at[v], fd.at[v], fs.at[v], ring1, fr_sem, v * 8)
              for v in (0, 1)]

    def part_of_first(k, v):
        rows = g[k * HALF:(k + 1) * HALF].reshape(rows_half, rows_all)
        for c in (0, 1):
            right = ab[1, c, :, :, v * PART:(v + 1) * PART].reshape(rows_all, PART)
            fp[v, k * HALF:(k + 1) * HALF, :, c * PART:(c + 1) * PART] = jnp.dot(
                rows, right, preferred_element_type=F32).astype(BF).reshape(HALF, ROWS, PART)

    for c in g_copies[0]:
        c.wait_recv()
    part_of_first(0, 0)
    for c in g_copies[1]:
        c.wait_recv()
    part_of_first(1, 0)
    next(firsts[0])
    part_of_first(0, 1)
    part_of_first(1, 1)
    next(firsts[1])
    gt[...] = g[...].reshape(rows_all, rows_all).T
    next(firsts[0])
    next(firsts[1])

    def both(way, ref):
        return ref.at[row_halves[way]]

    gathers = []
    for v in (0, 1):
        first[v] = next(firsts[v])
        f[v, own1] = first[v].astype(BF)
        gathers.append(gather(lambda d, v=v: f.at[v, place1(d)], ring1, f_sem, v * 8, both))
        next(gathers[v])
    next(gathers[0])
    next(gathers[1])

    seconds = [scatter(sp.at[v], pos2, (0, 1), sb.at[v], sh.at[v], sd.at[v], ss.at[v], ring2, sr_sem, v * 8)
               for v in (0, 1)]
    for v in (0, 1):
        next(gathers[v])
        second = 2.0315 * jnp.dot(gt[...], f[v].reshape(rows_all, COLS), preferred_element_type=F32)

        @pl.when(o == 0)
        def _():
            for t in range(N):
                for c in (0, 1):
                    part = second[t * ROWS:(t + 1) * ROWS, c * PART:(c + 1) * PART]
                    sp[v, t, c] = part.astype(BF)
            for c in (0, 1):
                sp[v, y, c] = (sp[v, y, c].astype(F32) - 4.775 * first[v, :, c * PART:(c + 1) * PART]).astype(BF)

        @pl.when(o == 1)
        def _():
            for t in range(N):
                for h in (0, 1):
                    at = ((t % NLO) * 2 + h) * ROWS
                    c = t // NLO
                    sp[v, t, h] = second[at:at + ROWS, c * PART:(c + 1) * PART].astype(BF)
            for c in (0, 1):
                at = c * NLO + z_lo
                sp[v, at, z_hi] = (
                    sp[v, at, z_hi].astype(F32) - 4.775 * first[v, :, c * PART:(c + 1) * PART]).astype(BF)

        next(seconds[v])
    next(seconds[0])
    for c in started[:-14]:
        c.wait_send()
    del started[:-14]
    next(seconds[1])

    def out_copy(v):
        return remote(ow.at[v, 1 - z_hi], o_ref.at[pl.ds(mine, ROWS), v * PART:(v + 1) * PART],
                      out_sem.at[0, v], out_sem.at[1, v], partner)

    for v in (0, 1):
        total = next(seconds[v])
        cols = slice(v * PART, (v + 1) * PART)

        @pl.when(o == 0)
        def _():
            for c in (0, 1):
                ow[v, c] = (3.4445 * ab[1, c, y, :, cols].astype(F32) + total[c]).astype(BF)
            out_copy(v).start()
            o_ref[pl.ds(mine, ROWS), cols] = ow[v, z_hi]

        @pl.when(o == 1)
        def _():
            for h in (0, 1):
                rows = slice(h * ROWS, (h + 1) * ROWS)
                o_ref[rows, cols] = (3.4445 * x_ref[rows, cols].astype(F32) + total[h]).astype(BF)

    for c in started:
        c.wait_send()

    @pl.when(o == 0)
    def _():
        for v in (0, 1):
            out_copy(v).wait()


def body(iterate):
    stack = pltpu.VMEM((2, N, ROWS, COLS), BF)
    gram = pltpu.VMEM((N, ROWS, N * ROWS), BF)
    chunks = lambda n: pltpu.VMEM((2, n, ROWS, COLS), BF)
    blocks = lambda n: pltpu.VMEM((2, n, 2, ROWS, PART), BF)
    dma = lambda n: pltpu.SemaphoreType.DMA((2, n))
    return pl.pallas_call(
        kernel,
        out_shape=jax.ShapeDtypeStruct(iterate.shape, BF),
        in_specs=[pl.BlockSpec(memory_space=pltpu.VMEM)],
        out_specs=pl.BlockSpec(memory_space=pltpu.VMEM),
        scratch_shapes=[
            pltpu.VMEM((2, 2, N, ROWS, COLS), BF),
            pltpu.VMEM((N * ROWS, N * ROWS), F32),
            gram, pltpu.VMEM((2, NX - 1, ROWS, N * ROWS), BF), gram,
            pltpu.VMEM((N * ROWS, N * ROWS), BF),
            stack,
            chunks(2), pltpu.VMEM((2, 2, ROWS // 2, COLS), BF), chunks(4), chunks(2),
            stack, pltpu.VMEM((2, ROWS, COLS), F32),
            blocks(N), blocks(2), pltpu.VMEM((2, 2, ROWS, PART), BF), blocks(4), blocks(2),
            pltpu.VMEM((2, 2, ROWS, PART), BF),
            dma(1), dma(16), dma(16), dma(6), dma(6), dma(16), dma(16), dma(16), dma(2),
        ],
        compiler_params=pltpu.CompilerParams(
            collective_id=0, has_side_effects=True, vmem_limit_bytes=40 * 1024 * 1024),
    )(iterate)


def solution(mesh):
    return jax.shard_map(
        body, mesh=mesh,
        in_specs=(P(("layer", "panel"), "col"),),
        out_specs=P(("layer", "panel"), "col"),
        check_vma=False,
    )
```

time: 469 us -> 84.3 us (0.18)
  the two profiles are of different devices: /device:TPU:6 before, /device:TPU:1 now
where the time goes in v3:
time: 84.3 us; the launch traced here: 84.2 us
  Pallas kernels  82.6 us (98%)
  local copies, waits for them, and re-layouts  1.56 us (2%)
    pallas_call x1, Pallas kernels, body(): pl.pallas_call(kernel, out_shape=jax.ShapeDtypeStruct(iterate.shape, BF),...  82.6 us

profile of v3, /device:TPU:1, one launch (start us, length us, event | category | flops | bytes accessed | tf_op | source)
XLA Modules:
  0.0 84.2 jit_solution(6195041484580060973)
XLA Ops:
  0.0 0.0 copy-start
  0.0 0.9 %copy-done = bf16[128,512]{1,0:T(8,128)(2,1)S(1)} copy-done((bf16[128,512]{1,0:T(8,128)(2,1)S(1)}, bf16[128,512]{1,0:T(8,128)(2,1)}, u32[]{:S(2)}) %copy-start) | copy-done | bytes 131096
  0.9 82.6 %shard_map.17 = bf16[128,512]{1,0:T(8,128)(2,1)S(1)} custom-call(bf16[128,512]{1,0:T(8,128)(2,1)S(1)} %copy-done), custom_call_target="tpu_custom_call" | custom-call | tf_op jit(solution)/shard_map/pallas_call | solution.py:294
  83.5 0.7 copy.3
Async XLA Ops:
  0.0 0.9 %copy-start = (bf16[128,512]{1,0:T(8,128)(2,1)S(1)}, bf16[128,512]{1,0:T(8,128)(2,1)}, u32[]{:S(2)}) copy-start(bf16[128,512]{1,0:T(8,128)(2,1)} %x_ref.1) | copy-start | bytes 393220

commit v4 on v3

--- a/solution.py
+++ b/solution.py
@@ -9,11 +9,13 @@
 HALF = N // 2
 ROWS, COLS = 64, 512
 PART = COLS // 2
+ORDER = ((4, 3, 5, 1), (7, 2, 6, 0))
+SLOT = {d: k * 4 + i for k in (0, 1) for i, d in enumerate(ORDER[k])}
 MESH = pl.DeviceIdType.MESH
 BF, F32 = jnp.bfloat16, jnp.float32
 
 
-def kernel(x_ref, o_ref, ab, acc, gp, gr, g, gt, fp, fb, fh, fd, fs, f, first, sp, sb, sh, sd, ss, ow,
+def kernel(x_hbm, o_ref, x_ref, x_sem, ab, acc, gp, gr, g, gt, fp, fb, fh, fd, fs, f, first, sp, sb, sh, sd, ss, ow,
            ex_sem, a_sem, b_sem, gr_sem, g_sem, fr_sem, f_sem, sr_sem, out_sem):
     panel, col, layer = lax.axis_index("panel"), lax.axis_index("col"), lax.axis_index("layer")
     y, z_lo = panel // NLO, panel % NLO
@@ -48,16 +50,17 @@
     def peer_x(d):
         return device((x + d) % NX, y, z)
 
-    own1 = place1(0)
     partner = device(x, y, (z + HALF) % N)
 
     barrier = pltpu.get_barrier_semaphore()
-    for d in range(1, N):
-        pl.semaphore_signal(barrier, inc=1, device_id=ring_y(d), device_id_type=MESH)
-        pl.semaphore_signal(barrier, inc=1, device_id=ring_z(d), device_id_type=MESH)
-    for d in range(1, NX):
-        pl.semaphore_signal(barrier, inc=1, device_id=peer_x(d), device_id_type=MESH)
-    pl.semaphore_wait(barrier, 2 * (N - 1) + NX - 1)
+    greeted = [device(x, y, (z + HALF) % N)] + [ring(d) for d in (2, -2, 1, -1) for ring in (ring_z, ring_y)]
+    greeted += [peer_x(d) for d in (2, 1, 3)]
+    for peer in greeted:
+        pl.semaphore_signal(barrier, inc=1, device_id=peer, device_id_type=MESH)
+    load = pltpu.make_async_copy(x_hbm, x_ref, x_sem)
+    load.start()
+    pl.semaphore_wait(barrier, len(greeted))
+    load.wait()
 
     def remote(src, dst, send_sem, recv_sem, to):
         return pltpu.make_async_remote_copy(
@@ -72,20 +75,19 @@
         return copy
 
     def gather(slot, ring, sems, base, far):
-        def one(code, src, d):
-            return send(src, src, sems.at[0, base + code], sems.at[1, base + code], ring(d))
-
-        own = slot(0)
-        second = [one(0, own, 2), one(1, own, -2)]
-        last = [one(2, own, 1), one(3, own, -1)]
+        def one(code, src, dst, d):
+            return send(src, dst, sems.at[0, base + code], sems.at[1, base + code], ring(d))
+
+        second = [one(0, slot(0, 0), slot(0, 2), 2), one(1, slot(0, 0), slot(0, -2), -2)]
+        last = [one(2, slot(0, 0), slot(0, 1), 1), one(3, slot(0, 0), slot(0, -1), -1)]
         yield
         for way, sign in ((0, 1), (1, -1)):
             second[way].wait_recv()
-            passed = slot(-2 * sign)
-            part = far(way, passed)
-            if part is not None:
-                last.append(one(4 + way, part, 2 * sign))
-            last.append(one(6 + way, passed, sign))
+            at = -2 * sign
+            src, dst = far(way, slot(at, 0)), far(way, slot(at, 2 * sign))
+            if src is not None:
+                last.append(one(4 + way, src, dst, 2 * sign))
+            last.append(one(6 + way, slot(at, 0), slot(at, sign), sign))
         yield
         for copy in last:
             copy.wait_recv()
@@ -100,9 +102,9 @@
             met.append([one(way, parts.at[index(4 * sign)].at[halves[way]], relay_half.at[way], 2 * sign)])
         for way, sign in ((0, -1), (1, 1)):
             met[way].append(one(2 + way, parts.at[index(3 * sign)], relay.at[way], sign))
-        for way, sign in ((0, -1), (1, 1)):
+        for way, sign in ((1, 1), (0, -1)):
             last.append(one(4 + way, parts.at[index(sign)], direct.at[way], sign))
-        yield
+            yield
         for way, sign in ((0, -1), (1, 1)):
             for copy in met[way]:
                 copy.wait_recv()
@@ -113,7 +115,7 @@
             last.append(one(6 + way, sums.at[way], direct.at[2 + way], 2 * sign))
         yield
         total = parts[index(0)].astype(F32)
-        for i, copy in enumerate(last):
+        for i, copy in zip((1, 0, 2, 3), last):
             copy.wait_recv()
             total += direct[i].astype(F32)
         yield total
@@ -124,22 +126,24 @@
     exchange = send(x_ref.at[pl.ds(other, ROWS), :], ab.at[1 - o, z_hi, y], ex_sem.at[0, 0], ex_sem.at[1, 0], partner)
 
     def slot_a(u):
-        def slot(d):
+        def slot(d, _):
             zz = (z + d + N) % N
             return ab.at[o, zz // NLO, (zz % NLO) * 2 + u]
         return slot
 
     def slot_b(c):
-        return lambda d: ab.at[1 - o, c, (y + d + N) % N]
-
-    def one_way(u):
-        return lambda way, ref: ref if way == u else None
+        return lambda d, _: ab.at[1 - o, c, (y + d + N) % N]
+
+    row_halves = (pl.ds(0, ROWS // 2), pl.ds(ROWS // 2, ROWS // 2))
+
+    def both(way, ref):
+        return ref.at[row_halves[way]]
 
     c_late = 1 - z_hi
-    a0 = gather(slot_a(0), ring_z, a_sem, 0, one_way(0))
-    a1 = gather(slot_a(1), ring_z, a_sem, 8, one_way(1))
-    b0 = gather(slot_b(z_hi), ring_y, b_sem, 0, one_way(0))
-    b1 = gather(slot_b(c_late), ring_y, b_sem, 8, one_way(1))
+    a0 = gather(slot_a(0), ring_z, a_sem, 0, lambda way, ref: None)
+    a1 = gather(slot_a(1), ring_z, a_sem, 8, lambda way, ref: None)
+    b0 = gather(slot_b(z_hi), ring_y, b_sem, 0, both)
+    b1 = gather(slot_b(c_late), ring_y, b_sem, 8, both)
     ab[1 - o, z_hi, y] = x_ref[pl.ds(mine, ROWS), :]
     next(b0)
     for u in (0, 1):
@@ -151,22 +155,33 @@
     exchange.wait_recv()
     next(b1)
     next(a1)
+    far = []
+    for way, sign in ((0, 1), (1, -1)):
+        zz, unseen = (z - 2 * sign + N) % N, 1 - (z + 2 * sign + N) % N // NLO
+        part = both(way, ab.at[o, zz // NLO, (zz % NLO) * 2 + unseen])
+        far.append(send(part, part, a_sem.at[0, 4 + way], a_sem.at[1, 4 + way], ring_z(2 * sign)))
+    ab[o, c_late, z_lo * 2 + z_hi] = ab[1 - o, c_late, y]
     next(b1)
     next(b0)
     next(a0)
     next(a1)
+    for copy in far:
+        copy.wait_recv()
 
     def nt(a, b):
         return lax.dot_general(a, b, (((1,), (1,)), ((), ())), preferred_element_type=F32)
 
     rows_all, rows_half = N * ROWS, HALF * ROWS
-    acc[...] = nt(ab[0, z_hi].reshape(rows_all, COLS), ab[1, z_hi].reshape(rows_all, COLS))
+    def left(k, c):
+        return jnp.concatenate([ab[0, c, place1(d)] for d in ORDER[k]], axis=0)
+
+    for k in (0, 1):
+        acc[k] = nt(left(k, z_hi), ab[1, z_hi].reshape(rows_all, COLS))
     next(b1)
 
     gr_copies = []
     for k in (0, 1):
-        block = acc[k * rows_half:(k + 1) * rows_half, :] + nt(
-            ab[0, c_late, k * HALF:(k + 1) * HALF].reshape(rows_half, COLS), ab[1, c_late].reshape(rows_all, COLS))
+        block = acc[k] + nt(left(k, c_late), ab[1, c_late].reshape(rows_all, COLS))
         gp[k * HALF:(k + 1) * HALF] = block.astype(BF).reshape(HALF, ROWS, rows_all)
         gr_copies.append([
             send(gp.at[k * HALF + (x + d) % NX], gr.at[k, d - 1], gr_sem.at[0, k * 3 + d - 1],
@@ -184,8 +199,7 @@
             send(g.at[mine_g], g.at[mine_g], g_sem.at[0, k * 3 + d - 1], g_sem.at[1, k * 3 + d - 1], peer_x(d))
             for d in (2, 1, 3)])
 
-    row_halves = (pl.ds(0, ROWS // 2), pl.ds(ROWS // 2, ROWS // 2))
-    firsts = [scatter(fp.at[v], place1, row_halves, fb.at[v], fh.at[v], fd.at[v], fs.at[v], ring1, fr_sem, v * 8)
+    firsts = [scatter(fp.at[v], lambda d: SLOT[d % N], row_halves, fb.at[v], fh.at[v], fd.at[v], fs.at[v], ring1, fr_sem, v * 8)
               for v in (0, 1)]
 
     def part_of_first(k, v):
@@ -195,28 +209,21 @@
             fp[v, k * HALF:(k + 1) * HALF, :, c * PART:(c + 1) * PART] = jnp.dot(
                 rows, right, preferred_element_type=F32).astype(BF).reshape(HALF, ROWS, PART)
 
-    for c in g_copies[0]:
-        c.wait_recv()
-    part_of_first(0, 0)
-    for c in g_copies[1]:
-        c.wait_recv()
-    part_of_first(1, 0)
-    next(firsts[0])
-    part_of_first(0, 1)
-    part_of_first(1, 1)
-    next(firsts[1])
+    for k in (0, 1):
+        for c in g_copies[k]:
+            c.wait_recv()
+        for v in (0, 1):
+            part_of_first(k, v)
+            next(firsts[v])
     gt[...] = g[...].reshape(rows_all, rows_all).T
     next(firsts[0])
     next(firsts[1])
 
-    def both(way, ref):
-        return ref.at[row_halves[way]]
-
     gathers = []
     for v in (0, 1):
         first[v] = next(firsts[v])
-        f[v, own1] = first[v].astype(BF)
-        gathers.append(gather(lambda d, v=v: f.at[v, place1(d)], ring1, f_sem, v * 8, both))
+        f[v, SLOT[0]] = first[v].astype(BF)
+        gathers.append(gather(lambda d, to, v=v: f.at[v, SLOT[(d - to) % N]], ring1, f_sem, v * 8, both))
         next(gathers[v])
     next(gathers[0])
     next(gathers[1])
@@ -249,6 +256,7 @@
                     sp[v, at, z_hi].astype(F32) - 4.775 * first[v, :, c * PART:(c + 1) * PART]).astype(BF)
 
         next(seconds[v])
+        next(seconds[v])
     next(seconds[0])
     for c in started[:-14]:
         c.wait_send()
@@ -294,11 +302,12 @@
     return pl.pallas_call(
         kernel,
         out_shape=jax.ShapeDtypeStruct(iterate.shape, BF),
-        in_specs=[pl.BlockSpec(memory_space=pltpu.VMEM)],
+        in_specs=[pl.BlockSpec(memory_space=pl.ANY)],
         out_specs=pl.BlockSpec(memory_space=pltpu.VMEM),
         scratch_shapes=[
+            pltpu.VMEM(iterate.shape, BF), pltpu.SemaphoreType.DMA(()),
             pltpu.VMEM((2, 2, N, ROWS, COLS), BF),
-            pltpu.VMEM((N * ROWS, N * ROWS), F32),
+            pltpu.VMEM((2, HALF * ROWS, N * ROWS), F32),
             gram, pltpu.VMEM((2, NX - 1, ROWS, N * ROWS), BF), gram,
             pltpu.VMEM((N * ROWS, N * ROWS), BF),
             stack,

time: 84.3 us -> 81.2 us (0.963)
  Pallas kernels: 82.6 us -> 79.3 us
    pallas_call x1, Pallas kernels: 82.6 us -> 79.3 us  [body(): pl.pallas_call(kernel, out_shape=jax.ShapeDtypeStruct(iterate.shape, BF),...]
where the time goes in v4:
time: 81.2 us; the launch traced here: 80.9 us
  Pallas kernels  79.3 us (98%)
  local copies, waits for them, and re-layouts  1.56 us (2%)
    pallas_call x1, Pallas kernels, body(): pl.pallas_call(kernel, out_shape=jax.ShapeDtypeStruct(iterate.shape, BF),...  79.3 us

profile of v4, /device:TPU:1, one launch (start us, length us, event | category | flops | bytes accessed | tf_op | source)
XLA Modules:
  0.0 80.9 jit_solution(17656410015231050387)
XLA Ops:
  0.0 0.0 copy-start
  0.0 0.9 %copy-done = bf16[128,512]{1,0:T(8,128)(2,1)S(1)} copy-done((bf16[128,512]{1,0:T(8,128)(2,1)S(1)}, bf16[128,512]{1,0:T(8,128)(2,1)}, u32[]{:S(2)}) %copy-start) | copy-done | bytes 131096
  0.9 79.3 %shard_map.17 = bf16[128,512]{1,0:T(8,128)(2,1)S(1)} custom-call(bf16[128,512]{1,0:T(8,128)(2,1)S(1)} %copy-done), custom_call_target="tpu_custom_call" | custom-call | tf_op jit(solution)/shard_map/pallas_call | solution.py:302
  80.2 0.7 copy.3
Async XLA Ops:
  0.0 0.9 %copy-start = (bf16[128,512]{1,0:T(8,128)(2,1)S(1)}, bf16[128,512]{1,0:T(8,128)(2,1)}, u32[]{:S(2)}) copy-start(bf16[128,512]{1,0:T(8,128)(2,1)} %x_hbm.1) | copy-start | bytes 393220

commit v5 on v4

--- a/solution.py
+++ b/solution.py
@@ -8,7 +8,8 @@
 NX, N, NLO = 4, 8, 4
 HALF = N // 2
 ROWS, COLS = 64, 512
-PART = COLS // 2
+PIECES = 4
+PART = COLS // PIECES
 ORDER = ((4, 3, 5, 1), (7, 2, 6, 0))
 SLOT = {d: k * 4 + i for k in (0, 1) for i, d in enumerate(ORDER[k])}
 MESH = pl.DeviceIdType.MESH
@@ -151,9 +152,9 @@
     next(a0)
     next(a1)
     next(b0)
-    next(a0)
     exchange.wait_recv()
     next(b1)
+    next(a0)
     next(a1)
     far = []
     for way, sign in ((0, 1), (1, -1)):
@@ -200,7 +201,7 @@
             for d in (2, 1, 3)])
 
     firsts = [scatter(fp.at[v], lambda d: SLOT[d % N], row_halves, fb.at[v], fh.at[v], fd.at[v], fs.at[v], ring1, fr_sem, v * 8)
-              for v in (0, 1)]
+              for v in range(PIECES)]
 
     def part_of_first(k, v):
         rows = g[k * HALF:(k + 1) * HALF].reshape(rows_half, rows_all)
@@ -212,27 +213,29 @@
     for k in (0, 1):
         for c in g_copies[k]:
             c.wait_recv()
-        for v in (0, 1):
+        for v in range(PIECES):
             part_of_first(k, v)
             next(firsts[v])
     gt[...] = g[...].reshape(rows_all, rows_all).T
-    next(firsts[0])
-    next(firsts[1])
+    for v in range(PIECES):
+        next(firsts[v])
+
 
     gathers = []
-    for v in (0, 1):
+    for v in range(PIECES):
         first[v] = next(firsts[v])
         f[v, SLOT[0]] = first[v].astype(BF)
         gathers.append(gather(lambda d, to, v=v: f.at[v, SLOT[(d - to) % N]], ring1, f_sem, v * 8, both))
         next(gathers[v])
-    next(gathers[0])
-    next(gathers[1])
+    for v in range(PIECES):
+        next(gathers[v])
+
 
     seconds = [scatter(sp.at[v], pos2, (0, 1), sb.at[v], sh.at[v], sd.at[v], ss.at[v], ring2, sr_sem, v * 8)
-               for v in (0, 1)]
-    for v in (0, 1):
+               for v in range(PIECES)]
+    for v in range(PIECES):
         next(gathers[v])
-        second = 2.0315 * jnp.dot(gt[...], f[v].reshape(rows_all, COLS), preferred_element_type=F32)
+        second = 2.0315 * jnp.dot(gt[...], f[v].reshape(rows_all, 2 * PART), preferred_element_type=F32)
 
         @pl.when(o == 0)
         def _():
@@ -257,17 +260,18 @@
 
         next(seconds[v])
         next(seconds[v])
-    next(seconds[0])
-    for c in started[:-14]:
+    for v in range(PIECES):
+        next(seconds[v])
+
+    for c in started[:-2 * PIECES]:
         c.wait_send()
-    del started[:-14]
-    next(seconds[1])
+    del started[:-2 * PIECES]
 
     def out_copy(v):
         return remote(ow.at[v, 1 - z_hi], o_ref.at[pl.ds(mine, ROWS), v * PART:(v + 1) * PART],
                       out_sem.at[0, v], out_sem.at[1, v], partner)
 
-    for v in (0, 1):
+    for v in range(PIECES):
         total = next(seconds[v])
         cols = slice(v * PART, (v + 1) * PART)
 
@@ -289,15 +293,15 @@
 
     @pl.when(o == 0)
     def _():
-        for v in (0, 1):
+        for v in range(PIECES):
             out_copy(v).wait()
 
 
 def body(iterate):
-    stack = pltpu.VMEM((2, N, ROWS, COLS), BF)
+    stack = pltpu.VMEM((PIECES, N, ROWS, 2 * PART), BF)
     gram = pltpu.VMEM((N, ROWS, N * ROWS), BF)
-    chunks = lambda n: pltpu.VMEM((2, n, ROWS, COLS), BF)
-    blocks = lambda n: pltpu.VMEM((2, n, 2, ROWS, PART), BF)
+    chunks = lambda n: pltpu.VMEM((PIECES, n, ROWS, 2 * PART), BF)
+    blocks = lambda n: pltpu.VMEM((PIECES, n, 2, ROWS, PART), BF)
     dma = lambda n: pltpu.SemaphoreType.DMA((2, n))
     return pl.pallas_call(
         kernel,
@@ -311,11 +315,11 @@
             gram, pltpu.VMEM((2, NX - 1, ROWS, N * ROWS), BF), gram,
             pltpu.VMEM((N * ROWS, N * ROWS), BF),
             stack,
-            chunks(2), pltpu.VMEM((2, 2, ROWS // 2, COLS), BF), chunks(4), chunks(2),
-            stack, pltpu.VMEM((2, ROWS, COLS), F32),
-            blocks(N), blocks(2), pltpu.VMEM((2, 2, ROWS, PART), BF), blocks(4), blocks(2),
-            pltpu.VMEM((2, 2, ROWS, PART), BF),
-            dma(1), dma(16), dma(16), dma(6), dma(6), dma(16), dma(16), dma(16), dma(2),
+            chunks(2), pltpu.VMEM((PIECES, 2, ROWS // 2, 2 * PART), BF), chunks(4), chunks(2),
+            stack, pltpu.VMEM((PIECES, ROWS, 2 * PART), F32),
+            blocks(N), blocks(2), pltpu.VMEM((PIECES, 2, ROWS, PART), BF), blocks(4), blocks(2),
+            pltpu.VMEM((PIECES, 2, ROWS, PART), BF),
+            dma(1), dma(16), dma(16), dma(6), dma(6), dma(8 * PIECES), dma(8 * PIECES), dma(8 * PIECES), dma(PIECES),
         ],
         compiler_params=pltpu.CompilerParams(
             collective_id=0, has_side_effects=True, vmem_limit_bytes=40 * 1024 * 1024),

time: 81.2 us -> 80.6 us (level)
  no operation moved by 1% of the time
where the time goes in v5:
time: 80.6 us; the launch traced here: 80.4 us
  Pallas kernels  78.9 us (98%)
  local copies, waits for them, and re-layouts  1.56 us (2%)
    pallas_call x1, Pallas kernels, body(): pl.pallas_call(kernel, out_shape=jax.ShapeDtypeStruct(iterate.shape, BF),...  78.9 us

profile of v5, /device:TPU:1, one launch (start us, length us, event | category | flops | bytes accessed | tf_op | source)
XLA Modules:
  0.0 80.4 jit_solution(16156749353725073811)
XLA Ops:
  0.0 0.0 copy-start
  0.0 0.9 %copy-done = bf16[128,512]{1,0:T(8,128)(2,1)S(1)} copy-done((bf16[128,512]{1,0:T(8,128)(2,1)S(1)}, bf16[128,512]{1,0:T(8,128)(2,1)}, u32[]{:S(2)}) %copy-start) | copy-done | bytes 131096
  0.9 78.9 %shard_map.17 = bf16[128,512]{1,0:T(8,128)(2,1)S(1)} custom-call(bf16[128,512]{1,0:T(8,128)(2,1)S(1)} %copy-done), custom_call_target="tpu_custom_call" | custom-call | tf_op jit(solution)/shard_map/pallas_call | solution.py:306
  79.8 0.7 copy.3
Async XLA Ops:
  0.0 0.9 %copy-start = (bf16[128,512]{1,0:T(8,128)(2,1)S(1)}, bf16[128,512]{1,0:T(8,128)(2,1)}, u32[]{:S(2)}) copy-start(bf16[128,512]{1,0:T(8,128)(2,1)} %x_hbm.1) | copy-start | bytes 393220

commit v6 on v5

--- a/solution.py
+++ b/solution.py
@@ -216,9 +216,9 @@
         for v in range(PIECES):
             part_of_first(k, v)
             next(firsts[v])
+            if k == 1:
+                next(firsts[v])
     gt[...] = g[...].reshape(rows_all, rows_all).T
-    for v in range(PIECES):
-        next(firsts[v])
 
 
     gathers = []

time: 80.6 us -> 79.5 us (0.986)
  Pallas kernels: 78.9 us -> 77.8 us
    pallas_call x1, Pallas kernels: 78.9 us -> 77.8 us  [body(): pl.pallas_call(kernel, out_shape=jax.ShapeDtypeStruct(iterate.shape, BF),...]
where the time goes in v6:
time: 79.5 us; the launch traced here: 79.4 us
  Pallas kernels  77.8 us (98%)
  local copies, waits for them, and re-layouts  1.56 us (2%)
    pallas_call x1, Pallas kernels, body(): pl.pallas_call(kernel, out_shape=jax.ShapeDtypeStruct(iterate.shape, BF),...  77.8 us

profile of v6, /device:TPU:1, one launch (start us, length us, event | category | flops | bytes accessed | tf_op | source)
XLA Modules:
  0.0 79.4 jit_solution(12336997987824811138)
XLA Ops:
  0.0 0.0 copy-start
  0.0 0.9 %copy-done = bf16[128,512]{1,0:T(8,128)(2,1)S(1)} copy-done((bf16[128,512]{1,0:T(8,128)(2,1)S(1)}, bf16[128,512]{1,0:T(8,128)(2,1)}, u32[]{:S(2)}) %copy-start) | copy-done | bytes 131096
  0.9 77.8 %shard_map.17 = bf16[128,512]{1,0:T(8,128)(2,1)S(1)} custom-call(bf16[128,512]{1,0:T(8,128)(2,1)S(1)} %copy-done), custom_call_target="tpu_custom_call" | custom-call | tf_op jit(solution)/shard_map/pallas_call | solution.py:306
  78.7 0.7 copy.3
Async XLA Ops:
  0.0 0.9 %copy-start = (bf16[128,512]{1,0:T(8,128)(2,1)S(1)}, bf16[128,512]{1,0:T(8,128)(2,1)}, u32[]{:S(2)}) copy-start(bf16[128,512]{1,0:T(8,128)(2,1)} %x_hbm.1) | copy-start | bytes 393220

commit v7 on v6

--- a/solution.py
+++ b/solution.py
@@ -218,7 +218,6 @@
             next(firsts[v])
             if k == 1:
                 next(firsts[v])
-    gt[...] = g[...].reshape(rows_all, rows_all).T
 
 
     gathers = []
@@ -227,6 +226,7 @@
         f[v, SLOT[0]] = first[v].astype(BF)
         gathers.append(gather(lambda d, to, v=v: f.at[v, SLOT[(d - to) % N]], ring1, f_sem, v * 8, both))
         next(gathers[v])
+    gt[...] = g[...].reshape(rows_all, rows_all).T
     for v in range(PIECES):
         next(gathers[v])
 

time: 79.5 us -> 79.5 us (level)
  no operation moved by 1% of the time
where the time goes in v7:
time: 79.5 us; the launch traced here: 79.4 us
  Pallas kernels  77.8 us (98%)
  local copies, waits for them, and re-layouts  1.56 us (2%)
    pallas_call x1, Pallas kernels, body(): pl.pallas_call(kernel, out_shape=jax.ShapeDtypeStruct(iterate.shape, BF),...  77.8 us

profile of v7, /device:TPU:1, one launch (start us, length us, event | category | flops | bytes accessed | tf_op | source)
XLA Modules:
  0.0 79.4 jit_solution(9195822088453243831)
XLA Ops:
  0.0 0.0 copy-start
  0.0 0.9 %copy-done = bf16[128,512]{1,0:T(8,128)(2,1)S(1)} copy-done((bf16[128,512]{1,0:T(8,128)(2,1)S(1)}, bf16[128,512]{1,0:T(8,128)(2,1)}, u32[]{:S(2)}) %copy-start) | copy-done | bytes 131096
  0.9 77.8 %shard_map.17 = bf16[128,512]{1,0:T(8,128)(2,1)S(1)} custom-call(bf16[128,512]{1,0:T(8,128)(2,1)S(1)} %copy-done), custom_call_target="tpu_custom_call" | custom-call | tf_op jit(solution)/shard_map/pallas_call | solution.py:306
  78.7 0.7 copy.3
Async XLA Ops:
  0.0 0.9 %copy-start = (bf16[128,512]{1,0:T(8,128)(2,1)S(1)}, bf16[128,512]{1,0:T(8,128)(2,1)}, u32[]{:S(2)}) copy-start(bf16[128,512]{1,0:T(8,128)(2,1)} %x_hbm.1) | copy-start | bytes 393220
